TPU v7x, 32 devices: a whole 2x2x4 slice. The times are simulated.
32 devices in a mesh: lon: 8 (over y, x, core), lat: 4 (over z).
Axes of the slice: x: 2, y: 2, z: 4, core: 2. Of those that a mesh axis runs over, the one named last changes fastest.
Arguments:
- state: float32 [75, 4, 64, 1024], P(None, None, 'lat', 'lon'), may hold values from -6 to 6
- depth_levels: int32 [64, 1024], P('lat', 'lon'), may hold values from 0 to 75, as said below
Outputs:
- new_state: float32 [75, 4, 64, 1024], P(None, None, 'lat', 'lon')
Inputs may be any that keep to these rules, and one draw needn't show every extreme that they name: `depth_levels`: the number of wet levels of each column; land (0) grows more common eastward.
All inputs are finite; a program needn't handle non-finite values.
Results may differ from a plain program's by a relative error of at most 0.000059.
Values sent between devices are 32-bit elements; how exact they have to be, the bound alone decides.
No kernel may reach another device: no remote copies, remote signals or barrier semaphores. Data moves between devices by JAX's collectives and lax.ppermute only.
A program may use at most 192 MiB of HBM per device.

v0:
```python
import functools

import jax
import jax.numpy as jnp
import numpy as np
from jax import lax
from jax.experimental import pallas as pl
from jax.experimental.pallas import tpu as pltpu
from jax.sharding import PartitionSpec as P

STEPS = 2
VERTICAL_MIX = 64.0
GROUP = 8
SUB = 8
PAD = 8
CHUNKS = 10
VMEM_LIMIT = 40 * 1024 * 1024


def elimination_table(levels):
    inside = np.zeros(levels)
    last = np.zeros(levels)
    upper = 0.0
    for k in range(levels):
        lower = VERTICAL_MIX if k else 0.0
        inside[k] = 1.0 / (1.0 + lower + VERTICAL_MIX - lower * upper)
        last[k] = 1.0 / (1.0 + lower - lower * upper)
        upper = VERTICAL_MIX * inside[k]
    return (np.stack([inside, last]) / 4).astype(np.float32)


def tile_pair(value, c, half):
    return value[c][half * SUB : (half + 1) * SUB, :]


def pack_columns(acc, values, slot, lane):
    for c in range(len(values)):
        for half in range(2):
            place = GROUP * slot + 2 * c + half
            turned = pltpu.roll(tile_pair(values, c, half), 2 * place + 1, axis=1)
            acc = jnp.where((lane >> 1) == place, turned, acc)
    return acc


def write_rows(state_ref, depth, outer_ref, inner_ref, channels, height, tiles=None):
    at_lat = lax.axis_index("lat")
    even = lax.rem(at_lat, 2) == 0
    fold = at_lat == lax.axis_size("lat") - 1
    shape = (SUB, 128)
    reverse = 127 - lax.broadcasted_iota(jnp.int32, shape, 1)
    line = lax.broadcasted_iota(jnp.int32, shape, 0)
    sign = jnp.where(lax.rem(line, channels) >= 2, -1.0, 1.0)
    rows = (state_ref.shape[0] - 2 * PAD) // height
    for start in tiles or range(0, rows, SUB):
        count = min(SUB, rows - start)
        at = pl.ds(start, SUB)
        base = PAD + start * height
        top = state_ref[pl.ds(base + height - 1, count, stride=height), :]
        bottom = state_ref[pl.ds(base, count, stride=height), :]
        if count < SUB:
            top = jnp.concatenate([top, jnp.broadcast_to(depth[-1:], (SUB - count, 128))], axis=0)
            bottom = jnp.concatenate([bottom, jnp.broadcast_to(depth[:1], (SUB - count, 128))], axis=0)
            sign = jnp.where(line >= count, 1.0, sign)
        mirrored = jnp.take_along_axis(top, reverse, axis=1) * sign
        outer_ref[at, :] = jnp.where(even, top, bottom)
        inner_ref[at, :] = jnp.where(even, bottom, jnp.where(fold, mirrored, top))


def zero_pads(ref):
    pad = jnp.zeros((PAD, 128), jnp.float32)
    ref[pl.ds(0, PAD), :] = pad
    ref[pl.ds(ref.shape[0] - PAD, PAD), :] = pad


def pack_kernel(levels, channels, height, state_hbm, levels_hbm, state_ref, depth_ref, columns_ref, outer_ref, inner_ref, levels_ref, sems):
    lane = lax.broadcasted_iota(jnp.int32, (SUB, 128), 1)
    level_rows = channels * height
    whole, rest = divmod(levels, GROUP)
    groups = whole + 1
    per_chunk = pl.cdiv(groups, CHUNKS)
    copies = []
    for n, first_group in enumerate(range(0, groups, per_chunk)):
        first_level = first_group * GROUP
        count = min(per_chunk * GROUP, levels - first_level) * level_rows
        copies.append(
            pltpu.make_async_copy(
                state_hbm.at[pl.ds(first_level * level_rows, count), :],
                state_ref.at[pl.ds(PAD + first_level * level_rows, count), :],
                sems.at[n],
            )
        )
    depth_copy = pltpu.make_async_copy(levels_hbm, levels_ref, sems.at[CHUNKS])
    depth_copy.start()
    for copy in copies:
        copy.start()
    zero_pads(state_ref)
    depth_copy.wait()
    depth = levels_ref[...].astype(jnp.float32)
    depth_ref[...] = depth
    empty = jnp.zeros((SUB, 128), jnp.float32)

    def group(g, count, acc):
        for slot in range(count):
            base = PAD + (g * GROUP + slot) * level_rows
            values = [state_ref[pl.ds(base + c * height, height), :] for c in range(channels)]
            acc = pack_columns(acc, values, slot, lane)
        columns_ref[g] = acc

    rows = levels * channels
    step = per_chunk * GROUP * channels
    for n, copy in enumerate(copies):
        copy.wait()
        for g in range(n * per_chunk, min((n + 1) * per_chunk, groups)):
            if g < whole:
                group(g, GROUP, empty)
            else:
                group(g, rest, pack_columns(empty, [depth], rest, lane))
        tiles = range(n * step, min((n + 1) * step, rows), SUB)
        write_rows(state_ref, depth, outer_ref, inner_ref, channels, height, tiles)


def interior_kernel(levels, channels, height, table_ref, state_ref, depth_ref, sum_ref, inverse_ref, pressure_ref):
    whole, rest = divmod(levels, GROUP)
    level_rows = channels * height
    full = (height, 128)
    column = lax.broadcasted_iota(jnp.int32, full, 1)
    row = lax.broadcasted_iota(jnp.int32, full, 0)
    at_west, at_east = column == 0, column == 127
    at_south, at_north = row == 0, row == height - 1
    at_lat = lax.axis_index("lat")
    total = height * lax.axis_size("lat")
    rotation = 0.4 + 1.6 * ((at_lat * height + row).astype(jnp.float32) + 0.5) / total
    depth = depth_ref[...]
    depth_east = jnp.where(at_east, 0.0, pltpu.roll(depth, 127, axis=1))
    depth_west = jnp.where(at_west, 0.0, pltpu.roll(depth, 1, axis=1))
    depth_north = jnp.where(at_north, 0.0, pltpu.roll(depth, height - 1, axis=0))
    depth_south = jnp.where(at_south, 0.0, pltpu.roll(depth, 1, axis=0))
    last_level = depth - 1.0
    slot_rows = height + 2 * PAD
    pad = jnp.zeros((PAD, 128), jnp.float32)
    for slot in range(GROUP):
        pressure_ref[pl.ds(slot * slot_rows, PAD), :] = pad
        pressure_ref[pl.ds(slot * slot_rows + PAD + height, PAD), :] = pad

    def group(g, count, pressure):
        for slot in range(count):
            k = g * GROUP + slot
            level = jnp.asarray(k, jnp.float32)
            inverse_ref[pl.ds(k * height, height), :] = jnp.where(
                last_level > level,
                table_ref[0, k],
                jnp.where(last_level == level, table_ref[1, k], 0.0),
            )
            base = PAD + (g * GROUP + slot) * level_rows

            def rows_at(c, shift):
                return state_ref[pl.ds(base + c * height + shift, height), :]

            values = [rows_at(c, 0) for c in range(channels)]
            pressure = pressure + jnp.where(depth > level, 0.3 * values[1] - 0.1 * values[0], 0.0)
            at = slot * slot_rows + PAD
            pressure_ref[pl.ds(at, height), :] = pressure
            slope_east = jnp.where(at_east, 0.0, pltpu.roll(pressure, 127, axis=1)) - jnp.where(
                at_west, 0.0, pltpu.roll(pressure, 1, axis=1)
            )
            slope_north = pressure_ref[pl.ds(at + 1, height), :] - pressure_ref[pl.ds(at - 1, height), :]
            east = [pltpu.roll(v, 127, axis=1) for v in values]
            west = [pltpu.roll(v, 1, axis=1) for v in values]
            north = [rows_at(c, 1) for c in range(channels)]
            south = [rows_at(c, -1) for c in range(channels)]
            weights = [
                jnp.where(d > level, 0.6, 0.0) for d in (depth_east, depth_west, depth_north, depth_south)
            ]
            from_east = jnp.where(at_east, 0.0, weights[0] - east[2])
            from_west = jnp.where(at_west, 0.0, weights[1] + west[2])
            from_north = jnp.where(at_north, 0.0, weights[2] - north[3])
            from_south = jnp.where(at_south, 0.0, weights[3] + south[3])
            centre = 4.0 - ((weights[0] + weights[1]) + (weights[2] + weights[3]))
            forces = [None, None, rotation * values[3] - slope_east, -rotation * values[2] - slope_north]
            for c in range(channels):
                moved = (centre * values[c] + from_east * east[c]) + (
                    from_west * west[c] + from_north * north[c]
                )
                moved = moved + from_south * south[c]
                if forces[c] is not None:
                    moved = moved + forces[c]
                sum_ref[pl.ds((g * GROUP + slot) * level_rows + c * height, height), :] = moved
        return pressure

    pressure = jnp.zeros(full, jnp.float32)
    for g in range(whole + 1):
        pressure = group(g, GROUP if g < whole else rest, pressure)


def halo_rows(levels, channels, height, state_ref, one_ref, two_ref, northern, out_ref):
    edge = height - 1 if northern else 0
    way = -1.0 if northern else 1.0

    at_lat = lax.axis_index("lat")
    even = lax.rem(at_lat, 2) == 0

    def halo(at, count, stride):
        one = one_ref[pl.ds(at, count, stride=stride), :]
        two = two_ref[pl.ds(at, count, stride=stride), :]
        if northern:
            return jnp.where(even, one, two)
        return jnp.where(even, jnp.where(at_lat == 0, 0.0, two), one)

    depth = halo(channels * levels, 1, 1)
    carry = jnp.zeros((1, 128), jnp.float32)
    for start in range(0, levels, SUB):
        count = min(SUB, levels - start)
        near = [halo(channels * start + c, count, channels) for c in range(channels)]
        level = lax.broadcasted_iota(jnp.int32, (count, 128), 0)
        wet = (level + start).astype(jnp.float32) < depth
        weight = jnp.where(wet, 0.6, 0.0)
        pressure = jnp.where(wet, 0.3 * near[1] - 0.1 * near[0], 0.0)
        if count < SUB:
            pressure = jnp.concatenate([pressure, jnp.zeros((SUB - count, 128), jnp.float32)], axis=0)
        level = lax.broadcasted_iota(jnp.int32, (SUB, 128), 0)
        for shift in (1, 2, 4):
            pressure = pressure + jnp.where(level >= shift, pltpu.roll(pressure, shift, axis=0), 0.0)
        pressure = pressure + carry
        carry = pressure[SUB - 1 : SUB, :]
        factor = weight + way * near[3]
        for c in range(channels):
            at = PAD + (start * channels + c) * height + edge
            own = state_ref[pl.ds(at, count, stride=channels * height), :]
            added = factor * near[c] - weight * own
            if c == 3:
                added = added + way * pressure[:count]
            out_ref[pl.ds(start * channels + c, count, stride=channels), :] = added


def halo_columns(levels, channels, own_ref, one_ref, two_ref, out_ref):
    assert channels == 4 and GROUP == 8
    shape = (SUB, 128)
    lane = lax.broadcasted_iota(jnp.int32, shape, 1)
    western = (lane & 1) == 1
    way = jnp.where(western, 1.0, -1.0)
    channel = (lane >> 2) & 3
    slot = lane >> 4

    even = lax.rem(lax.axis_index("lon"), 2) == 0

    def halo(g):
        one, two = one_ref[g], two_ref[g]
        east = jnp.where(even, one, two)
        west = jnp.where(even, two, one)
        return jnp.where(western, pltpu.roll(west, 1, axis=1), pltpu.roll(east, 127, axis=1))

    whole, rest = divmod(levels, GROUP)
    groups = whole + 1
    near = [halo(g) for g in range(groups)]
    depth = jnp.where(lane >> 2 == channels * rest, near[whole], 0.0)
    for shift in (4, 8, 16, 32, 64):
        depth = depth + pltpu.roll(depth, shift, axis=1)
    carry = jnp.zeros(shape, jnp.float32)
    for g in range(groups):
        wet = (slot + g * GROUP).astype(jnp.float32) < depth
        weight = jnp.where(wet, 0.6, 0.0)
        velocity = jnp.where(channel == 2, near[g], 0.0)
        velocity = velocity + pltpu.roll(velocity, 4, axis=1)
        velocity = velocity + pltpu.roll(velocity, 120, axis=1)
        pressure = 0.3 * pltpu.roll(near[g], 124, axis=1) - 0.1 * near[g]
        pressure = jnp.where(jnp.logical_and(wet, channel == 0), pressure, 0.0)
        pressure = pltpu.roll(pressure, 8, axis=1)
        for shift in (1, 2, 4):
            pressure = pressure + jnp.where(slot >= shift, pltpu.roll(pressure, 16 * shift, axis=1), 0.0)
        last = jnp.where(slot == GROUP - 1, pressure, 0.0)
        for shift in (16, 32, 64):
            last = last + pltpu.roll(last, shift, axis=1)
        pressure = pressure + carry
        carry = carry + last
        out_ref[g] = (weight + way * velocity) * near[g] - weight * own_ref[g] + way * pressure


def finish_kernel(
    last_step, levels, channels, height, state_ref, sum_ref, inverse_ref, depth_ref, own_ref, lon_one_ref, lon_two_ref, two_ref, one_ref, *refs
):
    if last_step:
        out_hbm, value_ref, north_ref, south_ref, edge_ref, sems = refs
    else:
        out_ref, columns_ref, outer_ref, inner_ref, value_ref, north_ref, south_ref, edge_ref = refs
        zero_pads(out_ref)
    whole, rest = divmod(levels, GROUP)
    level_rows = channels * height
    full = (height, 128)
    lane = lax.broadcasted_iota(jnp.int32, (SUB, 128), 1)
    row = lax.broadcasted_iota(jnp.int32, (SUB, 128), 0)
    at_edge = jnp.logical_or(lane == 0, lane == 127)
    at_south, at_north = row == 0, row == SUB - 1
    depth = depth_ref[...]
    halo_columns(levels, channels, own_ref, lon_one_ref, lon_two_ref, edge_ref)
    halo_rows(levels, channels, height, state_ref, one_ref, two_ref, True, north_ref)
    halo_rows(levels, channels, height, state_ref, one_ref, two_ref, False, south_ref)

    def forward(g, count, chosen, carried):
        edges = edge_ref[g]
        for slot in range(count):
            k = g * GROUP + slot
            inverse = inverse_ref[pl.ds(k * height, height), :]
            ratio = 4.0 * VERTICAL_MIX * inverse
            following = []
            for c, before in zip(chosen, carried):
                row = channels * k + c
                halves = []
                for half, (ref, at_row) in enumerate(((south_ref, at_south), (north_ref, at_north))):
                    at = pl.ds(k * level_rows + c * height + half * SUB, SUB)
                    place = GROUP * slot + 2 * c + half
                    columns = pltpu.roll(edges, 128 - (2 * place + 1), axis=1)
                    added = jnp.where(at_edge, columns, 0.0) + jnp.where(at_row, ref[pl.ds(row, 1), :], 0.0)
                    halves.append(sum_ref[at, :] + added)
                value = jnp.concatenate(halves, axis=0) * inverse - ratio * before
                value_ref[k, pl.ds(c * height, height), :] = value
                following.append(value)
            carried = tuple(following)
        return carried

    def out_copy(g, count, chosen, n):
        at = (pl.ds(g * GROUP, count), pl.ds(chosen[0] * height, len(chosen) * height))
        return pltpu.make_async_copy(value_ref.at[at], out_hbm.at[at], sems.at[n, g])

    def backward(g, count, chosen, solved, acc):
        for slot in reversed(range(count)):
            k = g * GROUP + slot
            upper = 4.0 * VERTICAL_MIX * inverse_ref[pl.ds(k * height, height), :]
            following = []
            for c, after in zip(chosen, solved):
                value = value_ref[k, pl.ds(c * height, height), :] - upper * after
                if last_step:
                    value_ref[k, pl.ds(c * height, height), :] = value
                else:
                    out_ref[pl.ds(PAD + k * level_rows + c * height, height), :] = value
                following.append(value)
            solved = tuple(following)
            if not last_step:
                acc = pack_columns(acc, solved, slot, lane)
        if not last_step:
            columns_ref[g] = acc
        return solved

    zero = jnp.zeros(full, jnp.float32)
    empty = jnp.zeros((SUB, 128), jnp.float32)
    passes = [(0, 1), (2, 3)] if last_step else [tuple(range(channels))]
    sizes = [GROUP] * whole + [rest]
    for n, chosen in enumerate(passes):
        carried = (zero,) * len(chosen)
        for g in range(whole + 1):
            carried = forward(g, sizes[g], chosen, carried)
        solved = (zero,) * len(chosen)
        for g in reversed(range(whole + 1)):
            acc = empty
            if not last_step and g == whole:
                acc = pack_columns(empty, [depth], rest, lane)
            solved = backward(g, sizes[g], chosen, solved, acc)
            if last_step:
                out_copy(g, sizes[g], chosen, n).start()
    if last_step:
        for n, chosen in enumerate(passes):
            for g in reversed(range(whole + 1)):
                out_copy(g, sizes[g], chosen, n).wait()
    else:
        write_rows(out_ref, depth, outer_ref, inner_ref, channels, height)


def in_vmem(count):
    return [pl.BlockSpec(memory_space=pltpu.VMEM)] * count


HBM = pl.BlockSpec(memory_space=pltpu.HBM)
PARAMS = pltpu.CompilerParams(vmem_limit_bytes=VMEM_LIMIT)


class Sizes:
    def __init__(self, shape):
        self.levels, self.channels, self.height, breadth = shape
        assert breadth == 128 and self.height == 2 * SUB and self.levels % GROUP
        self.own = (self.levels, self.channels, self.height)
        self.rows = self.levels * self.channels * self.height
        self.state = jax.ShapeDtypeStruct((self.rows + 2 * PAD, 128), jnp.float32)
        self.flat = jax.ShapeDtypeStruct((self.rows, 128), jnp.float32)
        self.solved = jax.ShapeDtypeStruct((self.levels, self.channels * self.height, 128), jnp.float32)
        self.depth = jax.ShapeDtypeStruct((self.height, 128), jnp.float32)
        self.inverse = jax.ShapeDtypeStruct((self.levels * self.height, 128), jnp.float32)
        self.columns = jax.ShapeDtypeStruct((self.levels // GROUP + 1, SUB, 128), jnp.float32)
        count = pl.cdiv(self.channels * self.levels + 1, SUB) * SUB
        self.edges = jax.ShapeDtypeStruct((count, 128), jnp.float32)
        self.messages = [self.columns, self.edges, self.edges]


def scratch(*shapes):
    return [pltpu.VMEM(s.shape, s.dtype) for s in shapes]


def pack(sizes, state, depth_levels):
    return pl.pallas_call(
        functools.partial(pack_kernel, *sizes.own),
        out_shape=[sizes.state, sizes.depth] + sizes.messages,
        in_specs=[HBM, HBM],
        out_specs=in_vmem(5),
        scratch_shapes=[pltpu.VMEM(sizes.depth.shape, jnp.int32), pltpu.SemaphoreType.DMA((CHUNKS + 1,))],
        compiler_params=PARAMS,
        name="pack",
    )(pltpu.with_memory_space_constraint(state, pltpu.HBM), pltpu.with_memory_space_constraint(depth_levels, pltpu.HBM))


def interior(sizes, table, state, depth):
    pressure = jax.ShapeDtypeStruct((GROUP * (sizes.height + 2 * PAD), 128), jnp.float32)
    return pl.pallas_call(
        functools.partial(interior_kernel, *sizes.own),
        out_shape=[sizes.flat, sizes.inverse],
        in_specs=[pl.BlockSpec(memory_space=pltpu.SMEM)] + in_vmem(2),
        out_specs=in_vmem(2),
        scratch_shapes=scratch(pressure),
        compiler_params=PARAMS,
        cost_estimate=pl.CostEstimate(flops=sizes.rows * 128 * 40, bytes_accessed=sizes.rows * 128 * 24, transcendentals=0),
        name="interior",
    )(table, state, depth)


def finish(sizes, last_step, state, summed, inverse, depth, own, lon_one, lon_two, one, two):
    if last_step:
        shapes, specs = sizes.solved, HBM
        extra = [pltpu.SemaphoreType.DMA((2, sizes.columns.shape[0]))]
    else:
        shapes, specs = [sizes.state] + sizes.messages, in_vmem(4)
        extra = []
    return pl.pallas_call(
        functools.partial(finish_kernel, last_step, *sizes.own),
        out_shape=shapes,
        in_specs=in_vmem(9),
        out_specs=specs,
        scratch_shapes=scratch(sizes.solved, sizes.edges, sizes.edges, sizes.columns) + extra,
        compiler_params=PARAMS,
        name="finish_last" if last_step else "finish",
    )(state, summed, inverse, depth, own, lon_one, lon_two, two, one)


def both_ways(pairs):
    return pairs + [(target, source) for source, target in pairs if target != source]


def exchange(columns, outer, inner):
    lons, lats = lax.axis_size("lon"), lax.axis_size("lat")

    def index(lon, lat):
        return lon * lats + lat

    outer_pairs, inner_pairs = [], []
    for lon in range(lons):
        outer_pairs += [(index(lon, lat), index(lon, lat + 1)) for lat in range(0, lats, 2)]
        inner_pairs += [(index(lon, lat), index(lon, lat + 1)) for lat in range(1, lats - 1, 2)]
        if lon < lons - 1 - lon:
            inner_pairs.append((index(lon, lats - 1), index(lons - 1 - lon, lats - 1)))
        if lon % 2 == 0:
            inner_pairs.append((index(lon, 0), index(lon + 1, 0)))
    two = lax.ppermute(inner, ("lon", "lat"), both_ways(inner_pairs))
    one = lax.ppermute(outer, ("lon", "lat"), both_ways(outer_pairs))
    lon_one = lax.ppermute(columns, "lon", both_ways([(i, i + 1) for i in range(0, lons, 2)]))
    lon_two = lax.ppermute(columns, "lon", both_ways([(i, (i + 1) % lons) for i in range(1, lons, 2)]))
    return lon_one, lon_two, one, two


def on_device(state, depth_levels):
    sizes = Sizes(state.shape)
    table = jnp.asarray(elimination_table(sizes.levels))
    current, depth, *messages = pack(sizes, state.reshape(sizes.flat.shape), depth_levels)
    for step_index in range(STEPS):
        last_step = step_index == STEPS - 1
        halos = exchange(*messages)
        summed, inverse = interior(sizes, table, current, depth)
        result = finish(sizes, last_step, current, summed, inverse, depth, messages[0], *halos)
        if not last_step:
            current, *messages = result
    return result.reshape(state.shape)


def solution(mesh):
    assert mesh.shape["lat"] % 2 == 0 and mesh.shape["lon"] % 2 == 0
    return jax.shard_map(
        on_device,
        mesh=mesh,
        in_specs=(P(None, None, "lat", "lon"), P("lat", "lon")),
        out_specs=P(None, None, "lat", "lon"),
        check_vma=False,
    )
```

profile of v0, /device:TPU:0, one launch (start us, length us, event | category | flops | bytes accessed | tf_op | source)
XLA Modules:
  0.0 25.9 jit_solution(6451413386931035234)
XLA Ops:
  0.0 0.0 copy-start
  0.0 2.5 %pack.1 = (f32[4816,128]{1,0:T(8,128)S(1)}, f32[16,128]{1,0:T(8,128)S(1)}, f32[10,8,128]{2,1,0:T(8,128)S(1)}, f32[304,128]{1,0:T(8,128)S(1)}, f32[304,128]{1,0:T(8,128)S(1)}) custom-call(f32[4800,128]{1,0:T(8,128)} %bitcast.2, s32[16,128]{1,0:T(8,128)} %levels_hbm.1), custom_call_target="tpu_custom_call" | custom-call | tf_op jit(solution)/shard_map/pack/pallas_call | solution.py:397
  2.5 0.5 %collective-permute-start.2 = (f32[304,128]{1,0:T(8,128)S(1)}, f32[304,128]{1,0:T(8,128)S(1)}, u32[]{:S(2)}, u32[]{:S(2)}) collective-permute-start(f32[304,128]{1,0:T(8,128)S(1)} %get-tuple-element.23), channel_id=1, source_target_pairs={{1,2},{3,31},{0,4},{5,6},{7,27},{9,10},{11,23},{8,12},{13,14},{15,... | collective-permute-start | bytes 466952 | tf_op jit(solution)/shard_map/ppermute | solution.py:458
  3.0 4.1 %collective-permute-start.3 = (f32[304,128]{1,0:T(8,128)S(1)}, f32[304,128]{1,0:T(8,128)S(1)}, u32[]{:S(2)}, u32[]{:S(2)}) collective-permute-start(f32[304,128]{1,0:T(8,128)S(1)} %get-tuple-element.24), channel_id=1, source_target_pairs={{0,1},{2,3},{4,5},{6,7},{8,9},{10,11},{12,13},{14,15},{16,17},{18,... | collective-permute-start | bytes 466952 | tf_op jit(solution)/shard_map/ppermute | solution.py:459
  7.1 1.3 %collective-permute-start.1 = (f32[10,8,128]{2,1,0:T(8,128)S(1)}, f32[10,8,128]{2,1,0:T(8,128)S(1)}, u32[]{:S(2)}, u32[]{:S(2)}) collective-permute-start(f32[10,8,128]{2,1,0:T(8,128)S(1)} %get-tuple-element.22.own_ref), channel_id=1, source_target_pairs={{4,8},{12,16},{20,24},{28,0},{8,4},{16,12},{24,20},{0,28},{5,9},{1... | collective-permute-start | bytes 122888 | tf_op jit(solution)/shard_map/ppermute | solution.py:461
  8.5 0.3 %collective-permute-start = (f32[10,8,128]{2,1,0:T(8,128)S(1)}, f32[10,8,128]{2,1,0:T(8,128)S(1)}, u32[]{:S(2)}, u32[]{:S(2)}) collective-permute-start(f32[10,8,128]{2,1,0:T(8,128)S(1)} %get-tuple-element.22.own_ref), channel_id=1, source_target_pairs={{0,4},{8,12},{16,20},{24,28},{4,0},{12,8},{20,16},{28,24},{1,5},{9... | collective-permute-start | bytes 122888 | tf_op jit(solution)/shard_map/ppermute | solution.py:460
  8.7 0.0 copy-done
  8.7 2.4 %interior.2 = (f32[4800,128]{1,0:T(8,128)S(1)}, f32[1200,128]{1,0:T(8,128)S(1)}) custom-call(f32[2,75]{1,0:T(2,128)S(1)} %copy-done, f32[4816,128]{1,0:T(8,128)S(1)} %get-tuple-element.18.state_ref, f32[16,128]{1,0:T(8,128)S(1)} %get-tuple-element.19.depth_ref), custom_call_target="tpu_custom_call" | custom-call | flops 24576000 | bytes 14745600 | tf_op jit(solution)/shard_map/interior/pallas_call | solution.py:410
  11.1 0.7 %collective-permute-done.1.lon_two_ref = f32[10,8,128]{2,1,0:T(8,128)S(1)} collective-permute-done((f32[10,8,128]{2,1,0:T(8,128)S(1)}, f32[10,8,128]{2,1,0:T(8,128)S(1)}, u32[]{:S(2)}, u32[]{:S(2)}) %collective-permute-start.1) | collective-permute-done | bytes 40992 | tf_op jit(solution)/shard_map/ppermute | solution.py:461
  11.8 0.0 collective-permute-done.lon_one_ref
  11.8 0.0 collective-permute-done.2.two_ref
  11.8 0.0 collective-permute-done.3.one_ref
  11.8 2.6 %finish.1 = (f32[4816,128]{1,0:T(8,128)S(1)}, f32[10,8,128]{2,1,0:T(8,128)S(1)}, f32[304,128]{1,0:T(8,128)S(1)}, f32[304,128]{1,0:T(8,128)S(1)}) custom-call(f32[4816,128]{1,0:T(8,128)S(1)} %get-tuple-element.18.state_ref, f32[4800,128]{1,0:T(8,128)S(1)} %get-tuple-element.20.sum_ref, f32[1200,128]{1,0:T(8,128)S(1)} %get-tuple-element.21.inverse_ref, ...), custom_call_target="tpu_custom_call" | custom-call | tf_op jit(solution)/shard_map/finish/pallas_call | solution.py:429
  14.4 0.1 collective-permute-start.6
  14.5 3.6 %collective-permute-start.7 = (f32[304,128]{1,0:T(8,128)S(1)}, f32[304,128]{1,0:T(8,128)S(1)}, u32[]{:S(2)}, u32[]{:S(2)}) collective-permute-start(f32[304,128]{1,0:T(8,128)S(1)} %get-tuple-element.30), channel_id=1, source_target_pairs={{0,1},{2,3},{4,5},{6,7},{8,9},{10,11},{12,13},{14,15},{16,17},{18,... | collective-permute-start | bytes 466952 | tf_op jit(solution)/shard_map/ppermute | solution.py:459
  18.2 0.0 collective-permute-start.5
  18.2 0.6 %collective-permute-start.4 = (f32[10,8,128]{2,1,0:T(8,128)S(1)}, f32[10,8,128]{2,1,0:T(8,128)S(1)}, u32[]{:S(2)}, u32[]{:S(2)}) collective-permute-start(f32[10,8,128]{2,1,0:T(8,128)S(1)} %get-tuple-element.28.own_ref), channel_id=1, source_target_pairs={{0,4},{8,12},{16,20},{24,28},{4,0},{12,8},{20,16},{28,24},{1,5},{9... | collective-permute-start | bytes 122888 | tf_op jit(solution)/shard_map/ppermute | solution.py:460
  18.8 2.4 %interior.3 = (f32[4800,128]{1,0:T(8,128)S(1)}, f32[1200,128]{1,0:T(8,128)S(1)}) custom-call(f32[2,75]{1,0:T(2,128)S(1)} %copy-done, f32[4816,128]{1,0:T(8,128)S(1)} %get-tuple-element.25.state_ref, f32[16,128]{1,0:T(8,128)S(1)} %get-tuple-element.19.depth_ref), custom_call_target="tpu_custom_call" | custom-call | flops 24576000 | bytes 14745600 | tf_op jit(solution)/shard_map/interior/pallas_call | solution.py:410
  21.2 1.3 %collective-permute-done.5.lon_two_ref = f32[10,8,128]{2,1,0:T(8,128)S(1)} collective-permute-done((f32[10,8,128]{2,1,0:T(8,128)S(1)}, f32[10,8,128]{2,1,0:T(8,128)S(1)}, u32[]{:S(2)}, u32[]{:S(2)}) %collective-permute-start.5) | collective-permute-done | bytes 40992 | tf_op jit(solution)/shard_map/ppermute | solution.py:461
  22.5 0.0 collective-permute-done.4.lon_one_ref
  22.5 0.0 collective-permute-done.6.two_ref
  22.5 0.0 collective-permute-done.7.one_ref
  22.5 3.4 %finish_last.1 = f32[75,64,128]{2,1,0:T(8,128)} custom-call(f32[4816,128]{1,0:T(8,128)S(1)} %get-tuple-element.25.state_ref, f32[4800,128]{1,0:T(8,128)S(1)} %get-tuple-element.26.sum_ref, f32[1200,128]{1,0:T(8,128)S(1)} %get-tuple-element.27.inverse_ref, f32[16,128]{1,0:T(8,128)S(1)} %get-tuple-element.19.depth_ref, ...), custom_call_target="tpu_custom_call" | custom-call | tf_op jit(solution)/shard_map/finish_last/pallas_call | solution.py:429
Async XLA Ops:
  0.0 8.7 %copy-start = (f32[2,75]{1,0:T(2,128)S(1)}, f32[2,75]{1,0:T(2,128)}, u32[]{:S(2)}) copy-start(f32[2,75]{1,0:T(2,128)} %constant.2.clone.table_ref) | copy-start | bytes 1804
  2.5 9.3 %collective-permute-start.2 = (f32[304,128]{1,0:T(8,128)S(1)}, f32[304,128]{1,0:T(8,128)S(1)}, u32[]{:S(2)}, u32[]{:S(2)}) collective-permute-start(f32[304,128]{1,0:T(8,128)S(1)} %get-tuple-element.23), channel_id=1, source_target_pairs={{1,2},{3,31},{0,4},{5,6},{7,27},{9,10},{11,23},{8,12},{13,14},{15,... | collective-permute-start | bytes 466952 | tf_op jit(solution)/shard_map/ppermute | solution.py:458
  3.0 8.8 %collective-permute-start.3 = (f32[304,128]{1,0:T(8,128)S(1)}, f32[304,128]{1,0:T(8,128)S(1)}, u32[]{:S(2)}, u32[]{:S(2)}) collective-permute-start(f32[304,128]{1,0:T(8,128)S(1)} %get-tuple-element.24), channel_id=1, source_target_pairs={{0,1},{2,3},{4,5},{6,7},{8,9},{10,11},{12,13},{14,15},{16,17},{18,... | collective-permute-start | bytes 466952 | tf_op jit(solution)/shard_map/ppermute | solution.py:459
  7.1 4.7 %collective-permute-start.1 = (f32[10,8,128]{2,1,0:T(8,128)S(1)}, f32[10,8,128]{2,1,0:T(8,128)S(1)}, u32[]{:S(2)}, u32[]{:S(2)}) collective-permute-start(f32[10,8,128]{2,1,0:T(8,128)S(1)} %get-tuple-element.22.own_ref), channel_id=1, source_target_pairs={{4,8},{12,16},{20,24},{28,0},{8,4},{16,12},{24,20},{0,28},{5,9},{1... | collective-permute-start | bytes 122888 | tf_op jit(solution)/shard_map/ppermute | solution.py:461
  8.5 3.3 %collective-permute-start = (f32[10,8,128]{2,1,0:T(8,128)S(1)}, f32[10,8,128]{2,1,0:T(8,128)S(1)}, u32[]{:S(2)}, u32[]{:S(2)}) collective-permute-start(f32[10,8,128]{2,1,0:T(8,128)S(1)} %get-tuple-element.22.own_ref), channel_id=1, source_target_pairs={{0,4},{8,12},{16,20},{24,28},{4,0},{12,8},{20,16},{28,24},{1,5},{9... | collective-permute-start | bytes 122888 | tf_op jit(solution)/shard_map/ppermute | solution.py:460
  14.4 8.0 %collective-permute-start.6 = (f32[304,128]{1,0:T(8,128)S(1)}, f32[304,128]{1,0:T(8,128)S(1)}, u32[]{:S(2)}, u32[]{:S(2)}) collective-permute-start(f32[304,128]{1,0:T(8,128)S(1)} %get-tuple-element.29), channel_id=1, source_target_pairs={{1,2},{3,31},{0,4},{5,6},{7,27},{9,10},{11,23},{8,12},{13,14},{15,... | collective-permute-start | bytes 466952 | tf_op jit(solution)/shard_map/ppermute | solution.py:458
  14.5 8.0 %collective-permute-start.7 = (f32[304,128]{1,0:T(8,128)S(1)}, f32[304,128]{1,0:T(8,128)S(1)}, u32[]{:S(2)}, u32[]{:S(2)}) collective-permute-start(f32[304,128]{1,0:T(8,128)S(1)} %get-tuple-element.30), channel_id=1, source_target_pairs={{0,1},{2,3},{4,5},{6,7},{8,9},{10,11},{12,13},{14,15},{16,17},{18,... | collective-permute-start | bytes 466952 | tf_op jit(solution)/shard_map/ppermute | solution.py:459
  18.2 4.3 %collective-permute-start.5 = (f32[10,8,128]{2,1,0:T(8,128)S(1)}, f32[10,8,128]{2,1,0:T(8,128)S(1)}, u32[]{:S(2)}, u32[]{:S(2)}) collective-permute-start(f32[10,8,128]{2,1,0:T(8,128)S(1)} %get-tuple-element.28.own_ref), channel_id=1, source_target_pairs={{4,8},{12,16},{20,24},{28,0},{8,4},{16,12},{24,20},{0,28},{5,9},{1... | collective-permute-start | bytes 122888 | tf_op jit(solution)/shard_map/ppermute | solution.py:461
  18.2 4.3 %collective-permute-start.4 = (f32[10,8,128]{2,1,0:T(8,128)S(1)}, f32[10,8,128]{2,1,0:T(8,128)S(1)}, u32[]{:S(2)}, u32[]{:S(2)}) collective-permute-start(f32[10,8,128]{2,1,0:T(8,128)S(1)} %get-tuple-element.28.own_ref), channel_id=1, source_target_pairs={{0,4},{8,12},{16,20},{24,28},{4,0},{12,8},{20,16},{28,24},{1,5},{9... | collective-permute-start | bytes 122888 | tf_op jit(solution)/shard_map/ppermute | solution.py:460
where the time goes:
time: 26 us; the launch traced here: 25.9 us
  Pallas kernels  13.2 us (51%)
  starting transfers between devices  10.6 us (41%)
  waiting for transfers between devices  2.01 us (8%)
    ppermute x2, starting transfers between devices, exchange(): one = lax.ppermute(outer, ('lon', 'lat'), both_ways(outer_pairs))  7.77 us
    pallas_call x2, Pallas kernels, finish(): pl.pallas_call(functools.partial(finish_kernel, last_step, *sizes.own), o...  6 us
    pallas_call x2, Pallas kernels, interior(): pl.pallas_call(functools.partial(interior_kernel, *sizes.own), out_shape=...  4.72 us
    pallas_call x1, Pallas kernels, pack(): pl.pallas_call(functools.partial(pack_kernel, *sizes.own), out_shape=[siz...  2.45 us
    ppermute x2, waiting for transfers between devices, exchange(): lax.ppermute(columns, 'lon', both_ways([(i, (i + 1) % lons) for i in rang...  1.99 us
    ppermute x2, starting transfers between devices, exchange(): lax.ppermute(columns, 'lon', both_ways([(i, (i + 1) % lons) for i in rang...  1.33 us
    ppermute x2, starting transfers between devices, exchange(): lax.ppermute(columns, 'lon', both_ways([(i, i + 1) for i in range(0, lons...  0.93 us
    ppermute x2, starting transfers between devices, exchange(): two = lax.ppermute(inner, ('lon', 'lat'), both_ways(inner_pairs))  0.59 us
  transfers between devices with their start and end apart: 8, of which 2 were waited for; matrix products, arithmetic and copies ran while one was open for 0% of the time, Pallas kernels for 18%

commit v1 on v0

--- a/solution.py
+++ b/solution.py
@@ -13,7 +13,7 @@
 GROUP = 8
 SUB = 8
 PAD = 8
-CHUNKS = 10
+CHUNKS = 5
 VMEM_LIMIT = 40 * 1024 * 1024
 
 
@@ -42,7 +42,7 @@
     return acc
 
 
-def write_rows(state_ref, depth, outer_ref, inner_ref, channels, height, tiles=None):
+def write_rows(state_ref, depth, outer_ref, inner_ref, channels, height):
     at_lat = lax.axis_index("lat")
     even = lax.rem(at_lat, 2) == 0
     fold = at_lat == lax.axis_size("lat") - 1
@@ -51,7 +51,7 @@
     line = lax.broadcasted_iota(jnp.int32, shape, 0)
     sign = jnp.where(lax.rem(line, channels) >= 2, -1.0, 1.0)
     rows = (state_ref.shape[0] - 2 * PAD) // height
-    for start in tiles or range(0, rows, SUB):
+    for start in range(0, rows, SUB):
         count = min(SUB, rows - start)
         at = pl.ds(start, SUB)
         base = PAD + start * height
@@ -72,23 +72,17 @@
     ref[pl.ds(ref.shape[0] - PAD, PAD), :] = pad
 
 
-def pack_kernel(levels, channels, height, state_hbm, levels_hbm, state_ref, depth_ref, columns_ref, outer_ref, inner_ref, levels_ref, sems):
-    lane = lax.broadcasted_iota(jnp.int32, (SUB, 128), 1)
+def pack_kernel(levels, channels, height, state_hbm, levels_hbm, state_ref, depth_ref, own_ref, one_ref, two_ref, outer_ref, inner_ref, levels_ref, sems):
     level_rows = channels * height
-    whole, rest = divmod(levels, GROUP)
-    groups = whole + 1
-    per_chunk = pl.cdiv(groups, CHUNKS)
+    per_chunk = 2 * GROUP
+    starts = range(0, levels, per_chunk)
     copies = []
-    for n, first_group in enumerate(range(0, groups, per_chunk)):
-        first_level = first_group * GROUP
-        count = min(per_chunk * GROUP, levels - first_level) * level_rows
-        copies.append(
-            pltpu.make_async_copy(
-                state_hbm.at[pl.ds(first_level * level_rows, count), :],
-                state_ref.at[pl.ds(PAD + first_level * level_rows, count), :],
-                sems.at[n],
-            )
-        )
+    assert len(starts) <= CHUNKS
+    for n, first in enumerate(starts):
+        count = min(per_chunk, levels - first) * level_rows
+        source = state_hbm.at[pl.ds(first * level_rows, count), :]
+        target = state_ref.at[pl.ds(PAD + first * level_rows, count), :]
+        copies.append(pltpu.make_async_copy(source, target, sems.at[n]))
     depth_copy = pltpu.make_async_copy(levels_hbm, levels_ref, sems.at[CHUNKS])
     depth_copy.start()
     for copy in copies:
@@ -97,26 +91,37 @@
     depth_copy.wait()
     depth = levels_ref[...].astype(jnp.float32)
     depth_ref[...] = depth
+    for n, copy in enumerate(copies):
+        copy.wait()
+        write_columns(levels, channels, height, state_ref, depth, own_ref, one_ref, two_ref, [n])
+    write_rows(state_ref, depth, outer_ref, inner_ref, channels, height)
+
+
+def write_columns(levels, channels, height, state_ref, depth, own_ref, one_ref, two_ref, halves=None):
+    lane = lax.broadcasted_iota(jnp.int32, (SUB, 128), 1)
+    odd_lane = (lane & 1) == 1
+    even = lax.rem(lax.axis_index("lon"), 2) == 0
+    whole, rest = divmod(levels, GROUP)
     empty = jnp.zeros((SUB, 128), jnp.float32)
 
-    def group(g, count, acc):
-        for slot in range(count):
-            base = PAD + (g * GROUP + slot) * level_rows
+    def group(g):
+        acc = empty
+        if g == whole:
+            acc = pack_columns(empty, [depth], rest, lane)
+        for slot in range(GROUP if g < whole else rest):
+            base = PAD + (g * GROUP + slot) * channels * height
             values = [state_ref[pl.ds(base + c * height, height), :] for c in range(channels)]
             acc = pack_columns(acc, values, slot, lane)
-        columns_ref[g] = acc
-
-    rows = levels * channels
-    step = per_chunk * GROUP * channels
-    for n, copy in enumerate(copies):
-        copy.wait()
-        for g in range(n * per_chunk, min((n + 1) * per_chunk, groups)):
-            if g < whole:
-                group(g, GROUP, empty)
-            else:
-                group(g, rest, pack_columns(empty, [depth], rest, lane))
-        tiles = range(n * step, min((n + 1) * step, rows), SUB)
-        write_rows(state_ref, depth, outer_ref, inner_ref, channels, height, tiles)
+        own_ref[g] = acc
+        return acc
+
+    for half in halves or reversed(range(pl.cdiv(whole + 1, 2))):
+        low = group(2 * half)
+        high = group(2 * half + 1) if 2 * half < whole else empty
+        first = jnp.where(odd_lane, low, pltpu.roll(high, 127, axis=1))
+        last = jnp.where(odd_lane, pltpu.roll(high, 1, axis=1), low)
+        one_ref[half] = jnp.where(even, last, first)
+        two_ref[half] = jnp.where(even, first, last)
 
 
 def interior_kernel(levels, channels, height, table_ref, state_ref, depth_ref, sum_ref, inverse_ref, pressure_ref):
@@ -244,10 +249,12 @@
     even = lax.rem(lax.axis_index("lon"), 2) == 0
 
     def halo(g):
-        one, two = one_ref[g], two_ref[g]
+        one, two = one_ref[g // 2], two_ref[g // 2]
         east = jnp.where(even, one, two)
         west = jnp.where(even, two, one)
-        return jnp.where(western, pltpu.roll(west, 1, axis=1), pltpu.roll(east, 127, axis=1))
+        if g % 2 == 0:
+            east, west = pltpu.roll(east, 127, axis=1), pltpu.roll(west, 1, axis=1)
+        return jnp.where(western, west, east)
 
     whole, rest = divmod(levels, GROUP)
     groups = whole + 1
@@ -276,12 +283,12 @@
 
 
 def finish_kernel(
-    last_step, levels, channels, height, state_ref, sum_ref, inverse_ref, depth_ref, own_ref, lon_one_ref, lon_two_ref, two_ref, one_ref, *refs
+    last_step, levels, channels, height, state_ref, sum_ref, inverse_ref, depth_ref, own_ref, lon_one_ref, lon_two_ref, one_ref, two_ref, *refs
 ):
     if last_step:
         out_hbm, value_ref, north_ref, south_ref, edge_ref, sems = refs
     else:
-        out_ref, columns_ref, outer_ref, inner_ref, value_ref, north_ref, south_ref, edge_ref = refs
+        out_ref, columns_ref, facing_one_ref, facing_two_ref, outer_ref, inner_ref, value_ref, north_ref, south_ref, edge_ref = refs
         zero_pads(out_ref)
     whole, rest = divmod(levels, GROUP)
     level_rows = channels * height
@@ -321,7 +328,7 @@
         at = (pl.ds(g * GROUP, count), pl.ds(chosen[0] * height, len(chosen) * height))
         return pltpu.make_async_copy(value_ref.at[at], out_hbm.at[at], sems.at[n, g])
 
-    def backward(g, count, chosen, solved, acc):
+    def backward(g, count, chosen, solved):
         for slot in reversed(range(count)):
             k = g * GROUP + slot
             upper = 4.0 * VERTICAL_MIX * inverse_ref[pl.ds(k * height, height), :]
@@ -334,14 +341,9 @@
                     out_ref[pl.ds(PAD + k * level_rows + c * height, height), :] = value
                 following.append(value)
             solved = tuple(following)
-            if not last_step:
-                acc = pack_columns(acc, solved, slot, lane)
-        if not last_step:
-            columns_ref[g] = acc
         return solved
 
     zero = jnp.zeros(full, jnp.float32)
-    empty = jnp.zeros((SUB, 128), jnp.float32)
     passes = [(0, 1), (2, 3)] if last_step else [tuple(range(channels))]
     sizes = [GROUP] * whole + [rest]
     for n, chosen in enumerate(passes):
@@ -350,10 +352,7 @@
             carried = forward(g, sizes[g], chosen, carried)
         solved = (zero,) * len(chosen)
         for g in reversed(range(whole + 1)):
-            acc = empty
-            if not last_step and g == whole:
-                acc = pack_columns(empty, [depth], rest, lane)
-            solved = backward(g, sizes[g], chosen, solved, acc)
+            solved = backward(g, sizes[g], chosen, solved)
             if last_step:
                 out_copy(g, sizes[g], chosen, n).start()
     if last_step:
@@ -361,6 +360,7 @@
             for g in reversed(range(whole + 1)):
                 out_copy(g, sizes[g], chosen, n).wait()
     else:
+        write_columns(levels, channels, height, out_ref, depth, columns_ref, facing_one_ref, facing_two_ref)
         write_rows(out_ref, depth, outer_ref, inner_ref, channels, height)
 
 
@@ -386,7 +386,8 @@
         self.columns = jax.ShapeDtypeStruct((self.levels // GROUP + 1, SUB, 128), jnp.float32)
         count = pl.cdiv(self.channels * self.levels + 1, SUB) * SUB
         self.edges = jax.ShapeDtypeStruct((count, 128), jnp.float32)
-        self.messages = [self.columns, self.edges, self.edges]
+        facing = jax.ShapeDtypeStruct((pl.cdiv(self.columns.shape[0], 2), SUB, 128), jnp.float32)
+        self.messages = [self.columns, facing, facing, self.edges, self.edges]
 
 
 def scratch(*shapes):
@@ -398,7 +399,7 @@
         functools.partial(pack_kernel, *sizes.own),
         out_shape=[sizes.state, sizes.depth] + sizes.messages,
         in_specs=[HBM, HBM],
-        out_specs=in_vmem(5),
+        out_specs=in_vmem(7),
         scratch_shapes=[pltpu.VMEM(sizes.depth.shape, jnp.int32), pltpu.SemaphoreType.DMA((CHUNKS + 1,))],
         compiler_params=PARAMS,
         name="pack",
@@ -424,7 +425,7 @@
         shapes, specs = sizes.solved, HBM
         extra = [pltpu.SemaphoreType.DMA((2, sizes.columns.shape[0]))]
     else:
-        shapes, specs = [sizes.state] + sizes.messages, in_vmem(4)
+        shapes, specs = [sizes.state] + sizes.messages, in_vmem(6)
         extra = []
     return pl.pallas_call(
         functools.partial(finish_kernel, last_step, *sizes.own),
@@ -434,14 +435,14 @@
         scratch_shapes=scratch(sizes.solved, sizes.edges, sizes.edges, sizes.columns) + extra,
         compiler_params=PARAMS,
         name="finish_last" if last_step else "finish",
-    )(state, summed, inverse, depth, own, lon_one, lon_two, two, one)
+    )(state, summed, inverse, depth, own, lon_one, lon_two, one, two)
 
 
 def both_ways(pairs):
     return pairs + [(target, source) for source, target in pairs if target != source]
 
 
-def exchange(columns, outer, inner):
+def exchange(lon_first, lon_second, outer, inner):
     lons, lats = lax.axis_size("lon"), lax.axis_size("lat")
 
     def index(lon, lat):
@@ -457,8 +458,8 @@
             inner_pairs.append((index(lon, 0), index(lon + 1, 0)))
     two = lax.ppermute(inner, ("lon", "lat"), both_ways(inner_pairs))
     one = lax.ppermute(outer, ("lon", "lat"), both_ways(outer_pairs))
-    lon_one = lax.ppermute(columns, "lon", both_ways([(i, i + 1) for i in range(0, lons, 2)]))
-    lon_two = lax.ppermute(columns, "lon", both_ways([(i, (i + 1) % lons) for i in range(1, lons, 2)]))
+    lon_one = lax.ppermute(lon_first, "lon", both_ways([(i, i + 1) for i in range(0, lons, 2)]))
+    lon_two = lax.ppermute(lon_second, "lon", both_ways([(i, (i + 1) % lons) for i in range(1, lons, 2)]))
     return lon_one, lon_two, one, two
 
 
@@ -468,9 +469,10 @@
     current, depth, *messages = pack(sizes, state.reshape(sizes.flat.shape), depth_levels)
     for step_index in range(STEPS):
         last_step = step_index == STEPS - 1
+        own, *messages = messages
         halos = exchange(*messages)
         summed, inverse = interior(sizes, table, current, depth)
-        result = finish(sizes, last_step, current, summed, inverse, depth, messages[0], *halos)
+        result = finish(sizes, last_step, current, summed, inverse, depth, own, *halos)
         if not last_step:
             current, *messages = result
     return result.reshape(state.shape)

time: 26 us -> 24.7 us (0.950)
  waiting for transfers between devices: 2.01 us -> 0.04 us
    ppermute x4, starting transfers between devices: 2.26 us -> 4.5 us  [the longest x2 3.48 us: exchange(): lax.ppermute(lon_second, 'lon', both_ways([(i, (i + 1) % lons) for i in r...]
    ppermute x4, waiting for transfers between devices: 2 us -> 0.03 us  [the longest x2 0.02 us: exchange(): lax.ppermute(lon_second, 'lon', both_ways([(i, (i + 1) % lons) for i in r...]
    ppermute x2, starting transfers between devices: 7.77 us -> 6.3 us  [exchange(): one = lax.ppermute(outer, ('lon', 'lat'), both_ways(outer_pairs))]
    ppermute x2, starting transfers between devices: 0.59 us -> 0.01 us  [exchange(): two = lax.ppermute(inner, ('lon', 'lat'), both_ways(inner_pairs))]
    pallas_call x2, Pallas kernels: 4.72 us -> 4.99 us  [interior(): pl.pallas_call(functools.partial(interior_kernel, *sizes.own), out_shape=...]
  transfers between devices with their start and end apart: 8 -> 8, of which waited for: 2 -> 0; matrix products, arithmetic and copies ran while one was open for 0% -> 0% of each run, Pallas kernels for 18% -> 21%
where the time goes in v1:
time: 24.7 us; the launch traced here: 24.3 us
  Pallas kernels  13.4 us (54%)
  starting transfers between devices  10.8 us (44%)
    ppermute x2, starting transfers between devices, exchange(): one = lax.ppermute(outer, ('lon', 'lat'), both_ways(outer_pairs))  6.3 us
    pallas_call x2, Pallas kernels, finish(): pl.pallas_call(functools.partial(finish_kernel, last_step, *sizes.own), o...  6.06 us
    pallas_call x2, Pallas kernels, interior(): pl.pallas_call(functools.partial(interior_kernel, *sizes.own), out_shape=...  4.99 us
    ppermute x2, starting transfers between devices, exchange(): lax.ppermute(lon_second, 'lon', both_ways([(i, (i + 1) % lons) for i in r...  3.48 us
    pallas_call x1, Pallas kernels, pack(): pl.pallas_call(functools.partial(pack_kernel, *sizes.own), out_shape=[siz...  2.37 us
    ppermute x2, starting transfers between devices, exchange(): lax.ppermute(lon_first, 'lon', both_ways([(i, i + 1) for i in range(0, lo...  1.01 us
  transfers between devices with their start and end apart: 8, of which 0 were waited for; matrix products, arithmetic and copies ran while one was open for 0% of the time, Pallas kernels for 21%

profile of v1, /device:TPU:0, one launch (start us, length us, event | category | flops | bytes accessed | tf_op | source)
XLA Modules:
  0.0 24.3 jit_solution(5875376857053146998)
XLA Ops:
  0.0 0.0 copy-start
  0.0 2.4 %pack.1 = (f32[4816,128]{1,0:T(8,128)S(1)}, f32[16,128]{1,0:T(8,128)S(1)}, f32[10,8,128]{2,1,0:T(8,128)S(1)}, f32[5,8,128]{2,1,0:T(8,128)S(1)}, f32[5,8,128]{2,1...) custom-call(f32[4800,128]{1,0:T(8,128)} %bitcast.2, s32[16,128]{1,0:T(8,128)} %levels_hbm.1), custom_call_target="tpu_custom_call" | custom-call | tf_op jit(solution)/shard_map/pack/pallas_call | solution.py:398
  2.4 3.1 %collective-permute-start.2 = (f32[304,128]{1,0:T(8,128)S(1)}, f32[304,128]{1,0:T(8,128)S(1)}, u32[]{:S(2)}, u32[]{:S(2)}) collective-permute-start(f32[304,128]{1,0:T(8,128)S(1)} %get-tuple-element.29), channel_id=1, source_target_pairs={{0,1},{2,3},{4,5},{6,7},{8,9},{10,11},{12,13},{14,15},{16,17},{18,... | collective-permute-start | bytes 466952 | tf_op jit(solution)/shard_map/ppermute | solution.py:460
  5.5 0.0 collective-permute-start.3
  5.5 0.5 %collective-permute-start = (f32[5,8,128]{2,1,0:T(8,128)S(1)}, f32[5,8,128]{2,1,0:T(8,128)S(1)}, u32[]{:S(2)}, u32[]{:S(2)}) collective-permute-start(f32[5,8,128]{2,1,0:T(8,128)S(1)} %get-tuple-element.27), channel_id=1, source_target_pairs={{0,4},{8,12},{16,20},{24,28},{4,0},{12,8},{20,16},{28,24},{1,5},{9... | collective-permute-start | bytes 61448 | tf_op jit(solution)/shard_map/ppermute | solution.py:461
  6.0 2.1 %collective-permute-start.1 = (f32[5,8,128]{2,1,0:T(8,128)S(1)}, f32[5,8,128]{2,1,0:T(8,128)S(1)}, u32[]{:S(2)}, u32[]{:S(2)}) collective-permute-start(f32[5,8,128]{2,1,0:T(8,128)S(1)} %get-tuple-element.28), channel_id=1, source_target_pairs={{4,8},{12,16},{20,24},{28,0},{8,4},{16,12},{24,20},{0,28},{5,9},{1... | collective-permute-start | bytes 61448 | tf_op jit(solution)/shard_map/ppermute | solution.py:462
  8.0 0.0 copy-done
  8.0 2.3 %interior.2 = (f32[4800,128]{1,0:T(8,128)S(1)}, f32[1200,128]{1,0:T(8,128)S(1)}) custom-call(f32[2,75]{1,0:T(2,128)S(1)} %copy-done, f32[4816,128]{1,0:T(8,128)S(1)} %get-tuple-element.22.state_ref, f32[16,128]{1,0:T(8,128)S(1)} %get-tuple-element.23.depth_ref), custom_call_target="tpu_custom_call" | custom-call | flops 24576000 | bytes 14745600 | tf_op jit(solution)/shard_map/interior/pallas_call | solution.py:411
  10.4 0.0 collective-permute-done.lon_one_ref
  10.4 0.0 collective-permute-done.1.lon_two_ref
  10.4 0.0 collective-permute-done.2.one_ref
  10.4 0.0 collective-permute-done.3.two_ref
  10.4 2.8 %finish.1 = (f32[4816,128]{1,0:T(8,128)S(1)}, f32[10,8,128]{2,1,0:T(8,128)S(1)}, f32[5,8,128]{2,1,0:T(8,128)S(1)}, f32[5,8,128]{2,1,0:T(8,128)S(1)}, f32[304,128]{1,0:T(8,128)S(1)}, /*index=5*/f32[304,128]{1,0:T(8,128)S(1)}) custom-call(f32[4816,128]{1,0:T(8,128)S(1)} %get-tuple-element.22.state_ref, f32[4800,128]{1,0:T(8,128)S(1)} %get-tuple-element.24.sum_ref, ...), custom_call_target="tpu_custom_call" | custom-call | tf_op jit(solution)/shard_map/finish/pallas_call | solution.py:430
  13.2 3.2 %collective-permute-start.6 = (f32[304,128]{1,0:T(8,128)S(1)}, f32[304,128]{1,0:T(8,128)S(1)}, u32[]{:S(2)}, u32[]{:S(2)}) collective-permute-start(f32[304,128]{1,0:T(8,128)S(1)} %get-tuple-element.37), channel_id=1, source_target_pairs={{0,1},{2,3},{4,5},{6,7},{8,9},{10,11},{12,13},{14,15},{16,17},{18,... | collective-permute-start | bytes 466952 | tf_op jit(solution)/shard_map/ppermute | solution.py:460
  16.4 0.0 collective-permute-start.7
  16.4 0.5 %collective-permute-start.4 = (f32[5,8,128]{2,1,0:T(8,128)S(1)}, f32[5,8,128]{2,1,0:T(8,128)S(1)}, u32[]{:S(2)}, u32[]{:S(2)}) collective-permute-start(f32[5,8,128]{2,1,0:T(8,128)S(1)} %get-tuple-element.35), channel_id=1, source_target_pairs={{0,4},{8,12},{16,20},{24,28},{4,0},{12,8},{20,16},{28,24},{1,5},{9... | collective-permute-start | bytes 61448 | tf_op jit(solution)/shard_map/ppermute | solution.py:461
  16.9 1.4 %collective-permute-start.5 = (f32[5,8,128]{2,1,0:T(8,128)S(1)}, f32[5,8,128]{2,1,0:T(8,128)S(1)}, u32[]{:S(2)}, u32[]{:S(2)}) collective-permute-start(f32[5,8,128]{2,1,0:T(8,128)S(1)} %get-tuple-element.36), channel_id=1, source_target_pairs={{4,8},{12,16},{20,24},{28,0},{8,4},{16,12},{24,20},{0,28},{5,9},{1... | collective-permute-start | bytes 61448 | tf_op jit(solution)/shard_map/ppermute | solution.py:462
  18.3 2.6 %interior.3 = (f32[4800,128]{1,0:T(8,128)S(1)}, f32[1200,128]{1,0:T(8,128)S(1)}) custom-call(f32[2,75]{1,0:T(2,128)S(1)} %copy-done, f32[4816,128]{1,0:T(8,128)S(1)} %get-tuple-element.31.state_ref, f32[16,128]{1,0:T(8,128)S(1)} %get-tuple-element.23.depth_ref), custom_call_target="tpu_custom_call" | custom-call | flops 24576000 | bytes 14745600 | tf_op jit(solution)/shard_map/interior/pallas_call | solution.py:411
  21.0 0.0 collective-permute-done.4.lon_one_ref
  21.0 0.0 collective-permute-done.5.lon_two_ref
  21.0 0.0 collective-permute-done.6.one_ref
  21.0 0.0 collective-permute-done.7.two_ref
  21.0 3.3 %finish_last.1 = f32[75,64,128]{2,1,0:T(8,128)} custom-call(f32[4816,128]{1,0:T(8,128)S(1)} %get-tuple-element.31.state_ref, f32[4800,128]{1,0:T(8,128)S(1)} %get-tuple-element.32.sum_ref, f32[1200,128]{1,0:T(8,128)S(1)} %get-tuple-element.33.inverse_ref, f32[16,128]{1,0:T(8,128)S(1)} %get-tuple-element.23.depth_ref, ...), custom_call_target="tpu_custom_call" | custom-call | tf_op jit(solution)/shard_map/finish_last/pallas_call | solution.py:430
Async XLA Ops:
  0.0 8.0 %copy-start = (f32[2,75]{1,0:T(2,128)S(1)}, f32[2,75]{1,0:T(2,128)}, u32[]{:S(2)}) copy-start(f32[2,75]{1,0:T(2,128)} %constant.2.clone.table_ref) | copy-start | bytes 1804
  2.4 8.0 %collective-permute-start.2 = (f32[304,128]{1,0:T(8,128)S(1)}, f32[304,128]{1,0:T(8,128)S(1)}, u32[]{:S(2)}, u32[]{:S(2)}) collective-permute-start(f32[304,128]{1,0:T(8,128)S(1)} %get-tuple-element.29), channel_id=1, source_target_pairs={{0,1},{2,3},{4,5},{6,7},{8,9},{10,11},{12,13},{14,15},{16,17},{18,... | collective-permute-start | bytes 466952 | tf_op jit(solution)/shard_map/ppermute | solution.py:460
  5.5 5.0 %collective-permute-start.3 = (f32[304,128]{1,0:T(8,128)S(1)}, f32[304,128]{1,0:T(8,128)S(1)}, u32[]{:S(2)}, u32[]{:S(2)}) collective-permute-start(f32[304,128]{1,0:T(8,128)S(1)} %get-tuple-element.30), channel_id=1, source_target_pairs={{1,2},{3,31},{0,4},{5,6},{7,27},{9,10},{11,23},{8,12},{13,14},{15,... | collective-permute-start | bytes 466952 | tf_op jit(solution)/shard_map/ppermute | solution.py:459
  5.5 4.9 %collective-permute-start = (f32[5,8,128]{2,1,0:T(8,128)S(1)}, f32[5,8,128]{2,1,0:T(8,128)S(1)}, u32[]{:S(2)}, u32[]{:S(2)}) collective-permute-start(f32[5,8,128]{2,1,0:T(8,128)S(1)} %get-tuple-element.27), channel_id=1, source_target_pairs={{0,4},{8,12},{16,20},{24,28},{4,0},{12,8},{20,16},{28,24},{1,5},{9... | collective-permute-start | bytes 61448 | tf_op jit(solution)/shard_map/ppermute | solution.py:461
  6.0 4.4 %collective-permute-start.1 = (f32[5,8,128]{2,1,0:T(8,128)S(1)}, f32[5,8,128]{2,1,0:T(8,128)S(1)}, u32[]{:S(2)}, u32[]{:S(2)}) collective-permute-start(f32[5,8,128]{2,1,0:T(8,128)S(1)} %get-tuple-element.28), channel_id=1, source_target_pairs={{4,8},{12,16},{20,24},{28,0},{8,4},{16,12},{24,20},{0,28},{5,9},{1... | collective-permute-start | bytes 61448 | tf_op jit(solution)/shard_map/ppermute | solution.py:462
  13.2 7.8 %collective-permute-start.6 = (f32[304,128]{1,0:T(8,128)S(1)}, f32[304,128]{1,0:T(8,128)S(1)}, u32[]{:S(2)}, u32[]{:S(2)}) collective-permute-start(f32[304,128]{1,0:T(8,128)S(1)} %get-tuple-element.37), channel_id=1, source_target_pairs={{0,1},{2,3},{4,5},{6,7},{8,9},{10,11},{12,13},{14,15},{16,17},{18,... | collective-permute-start | bytes 466952 | tf_op jit(solution)/shard_map/ppermute | solution.py:460
  16.4 4.6 %collective-permute-start.7 = (f32[304,128]{1,0:T(8,128)S(1)}, f32[304,128]{1,0:T(8,128)S(1)}, u32[]{:S(2)}, u32[]{:S(2)}) collective-permute-start(f32[304,128]{1,0:T(8,128)S(1)} %get-tuple-element.38), channel_id=1, source_target_pairs={{1,2},{3,31},{0,4},{5,6},{7,27},{9,10},{11,23},{8,12},{13,14},{15,... | collective-permute-start | bytes 466952 | tf_op jit(solution)/shard_map/ppermute | solution.py:459
  16.4 4.6 %collective-permute-start.4 = (f32[5,8,128]{2,1,0:T(8,128)S(1)}, f32[5,8,128]{2,1,0:T(8,128)S(1)}, u32[]{:S(2)}, u32[]{:S(2)}) collective-permute-start(f32[5,8,128]{2,1,0:T(8,128)S(1)} %get-tuple-element.35), channel_id=1, source_target_pairs={{0,4},{8,12},{16,20},{24,28},{4,0},{12,8},{20,16},{28,24},{1,5},{9... | collective-permute-start | bytes 61448 | tf_op jit(solution)/shard_map/ppermute | solution.py:461
  16.9 4.1 %collective-permute-start.5 = (f32[5,8,128]{2,1,0:T(8,128)S(1)}, f32[5,8,128]{2,1,0:T(8,128)S(1)}, u32[]{:S(2)}, u32[]{:S(2)}) collective-permute-start(f32[5,8,128]{2,1,0:T(8,128)S(1)} %get-tuple-element.36), channel_id=1, source_target_pairs={{4,8},{12,16},{20,24},{28,0},{8,4},{16,12},{24,20},{0,28},{5,9},{1... | collective-permute-start | bytes 61448 | tf_op jit(solution)/shard_map/ppermute | solution.py:462
